TPU v7x, 32 devices: a whole 2x2x4 slice. The times are simulated.
32 devices in a mesh: dp: 4 (over z), fsdp: 8 (over y, x, core).
Axes of the slice: x: 2, y: 2, z: 4, core: 2. Of those that a mesh axis runs over, the one named last changes fastest.
Arguments:
- activations: bfloat16 [64, 256, 1024], P(('dp', 'fsdp')), may hold values from -6 to 6
- lengths: int32 [64, 4], P(('dp', 'fsdp')), may hold values from 1 to 128, 256 in all within a row
- cotangent: bfloat16 [64, 256, 1024], P(('dp', 'fsdp')), may hold values from -8 to 8
- gain_first: float32 [1024], replicated, may hold values from 0.5 to 1.5
- shift_first: float32 [1024], replicated, may hold values from -1 to 1
- triple_weight: bfloat16 [1024, 3072], P('fsdp', 'dp'), may hold values from -0.1875 to 0.1875
- output_weight: bfloat16 [1024, 1024], P('fsdp', 'dp'), may hold values from -0.5 to 0.5
- output_bias: float32 [1024], replicated, may hold values from -1.5 to 1.5
- gain_second: float32 [1024], replicated, may hold values from 0.5 to 1.5
- shift_second: float32 [1024], replicated, may hold values from -1 to 1
- upward_weight: bfloat16 [1024, 4096], P('fsdp', 'dp'), may hold values from -0.1875 to 0.1875
- upward_bias: float32 [4096], replicated, may hold values from -1.5 to 1.5
- downward_weight: bfloat16 [4096, 1024], P('fsdp', 'dp'), may hold values from -0.09375 to 0.09375
- downward_bias: float32 [1024], replicated, may hold values from -1.5 to 1.5
- prefix_table: bfloat16 [10, 1024], replicated, may hold values from -5 to 5
- inner_weight: bfloat16 [1024, 512], replicated, may hold values from -0.1875 to 0.1875
- inner_bias: float32 [512], replicated, may hold values from -1.5 to 1.5
- outer_weight: bfloat16 [512, 2048], replicated, may hold values from -0.25 to 0.25
- outer_bias: float32 [2048], replicated, may hold values from -1.5 to 1.5
Outputs:
- block_output: bfloat16 [64, 256, 1024], P(('dp', 'fsdp'))
- input_grad: bfloat16 [64, 256, 1024], P(('dp', 'fsdp'))
- table_grad: float32 [10, 1024], replicated
- inner_weight_grad: float32 [1024, 512], replicated
- inner_bias_grad: float32 [512], replicated
- outer_weight_grad: float32 [512, 2048], replicated
- outer_bias_grad: float32 [2048], replicated
Inputs may be any that keep to these rules, and one draw needn't show every extreme that they name: The 4 lengths of a row sum to 256, and some row's longest document has exactly 128 tokens.
All inputs are finite; a program needn't handle non-finite values.
Results may differ from a plain program's by a relative error of at most 0.011.
Values may be sent and summed in bfloat16 or wider, within the bound.
No kernel may reach another device: no remote copies, remote signals or barrier semaphores. Data moves between devices by JAX's collectives and lax.ppermute only.
A program may use at most 192 MiB of HBM per device.

v0:
```python
from functools import partial

import jax
import jax.numpy as jnp
from jax import lax
from jax.sharding import PartitionSpec as P

HEAD = 64


HIGHEST = lax.Precision.HIGHEST
masked_score = -1e30


def collect(triple_weight, output_weight, upward_weight, downward_weight):
    by_rows = (
        lax.all_gather(triple_weight, "fsdp", axis=0, tiled=True),
        lax.all_gather(output_weight, "fsdp", axis=0, tiled=True),
        lax.all_gather(upward_weight, "fsdp", axis=0, tiled=True),
        lax.all_gather(downward_weight, "fsdp", axis=0, tiled=True),
    )
    return (
        lax.all_gather(by_rows[0], "dp", axis=1, tiled=True),
        lax.all_gather(by_rows[1], "dp", axis=1, tiled=True),
        lax.all_gather(by_rows[2], "dp", axis=1, tiled=True),
        lax.all_gather(by_rows[3], "dp", axis=1, tiled=True),
    )


def normalize(values, scaling, offset):
    center = values - jnp.mean(values, axis=-1, keepdims=True)
    scaled = lax.rsqrt(jnp.mean(center * center, axis=-1, keepdims=True) + 1e-05)
    unit_rows = center * scaled
    return (unit_rows * scaling + offset, unit_rows, scaled)


def norm_back(upstream, unit_rows, scaled, scaling):
    scaled_up = upstream * scaling
    return scaled * (
        scaled_up
        - jnp.mean(scaled_up, axis=-1, keepdims=True)
        - unit_rows * jnp.mean(scaled_up * unit_rows, axis=-1, keepdims=True)
    )


def visibility(lengths_row, length, prefix):
    bounds = jnp.cumsum(lengths_row)
    places = jnp.arange(length, dtype=jnp.int32)
    segment = jnp.sum((places[:, None] >= bounds[None, :]).astype(jnp.int32), axis=1)
    within = (segment[:, None] == segment[None, :]) & (places[:, None] >= places[None, :])
    return jnp.concatenate([jnp.ones((length, prefix), jnp.int32) > 0, within], axis=1)


def attend_scores(queries, keys_all, visible, score_scale):
    scores = (
        jnp.einsum("qhe,khe->hqk", queries, keys_all, preferred_element_type=jnp.float32)
        * score_scale
    )
    return jnp.where(visible[None], scores, masked_score)


def forward_row(packed, visible, prefix_pair, weights, smalls, score_scale):
    triple_w, output_w, upward_w, downward_w = weights
    gain_one, shift_one, output_b, gain_two, shift_two, upward_b, downward_b = smalls
    length = packed.shape[0]
    model_width = packed.shape[1]
    head_count = model_width // HEAD
    start_rows = packed.astype(jnp.float32)
    normed, unit_one, scale_one = normalize(start_rows, gain_one, shift_one)
    triple = jnp.dot(
        normed.astype(jnp.bfloat16), triple_w, preferred_element_type=jnp.float32
    ).astype(jnp.bfloat16)
    queries = triple[:, :model_width].reshape(length, head_count, HEAD)
    keys_all = jnp.concatenate(
        [
            prefix_pair[0],
            triple[:, model_width : 2 * model_width].reshape(length, head_count, HEAD),
        ],
        0,
    )
    values_all = jnp.concatenate(
        [prefix_pair[1], triple[:, 2 * model_width :].reshape(length, head_count, HEAD)], 0
    )
    scores = attend_scores(queries, keys_all, visible, score_scale)
    maxima = jnp.max(scores, axis=-1, keepdims=True)
    totals = jnp.sum(jnp.exp(scores - maxima), axis=-1, keepdims=True)
    log_total = maxima + jnp.log(totals)
    attention = jnp.exp(scores - log_total).astype(jnp.bfloat16)
    mixture = jnp.einsum("hqk,khe->qhe", attention, values_all, preferred_element_type=jnp.float32)
    mixture = mixture.reshape(length, model_width).astype(jnp.bfloat16)
    middle = start_rows + jnp.dot(mixture, output_w, preferred_element_type=jnp.float32) + output_b
    normed_two, unit_two, scale_two = normalize(middle, gain_two, shift_two)
    upward = (
        jnp.dot(normed_two.astype(jnp.bfloat16), upward_w, preferred_element_type=jnp.float32)
        + upward_b
    )
    active = jax.nn.gelu(upward, approximate=True).astype(jnp.bfloat16)
    result = middle + jnp.dot(active, downward_w, preferred_element_type=jnp.float32) + downward_b
    saved_state = (
        unit_one,
        scale_one,
        queries,
        keys_all,
        values_all,
        log_total,
        unit_two,
        scale_two,
        upward,
    )
    return (result, saved_state)


def backward_row(upstream, saved_state, visible, weights, smalls, score_scale, prefix):
    triple_w, output_w, upward_w, downward_w = weights
    gain_one, shift_one, output_b, gain_two, shift_two, upward_b, downward_b = smalls
    unit_one, scale_one, queries, keys_all, values_all, log_total, unit_two, scale_two, upward = (
        saved_state
    )
    length = upstream.shape[0]
    model_width = upstream.shape[1]
    head_count = model_width // HEAD
    down_grad = upstream.astype(jnp.bfloat16)
    active_grad = jnp.einsum("td,fd->tf", down_grad, downward_w, preferred_element_type=jnp.float32)
    gelu_value, gelu_back = jax.vjp(partial(jax.nn.gelu, approximate=True), upward)
    upward_grad = gelu_back(active_grad)[0].astype(jnp.bfloat16)
    second_grad = jnp.einsum("tf,df->td", upward_grad, upward_w, preferred_element_type=jnp.float32)
    middle_grad = upstream + norm_back(second_grad, unit_two, scale_two, gain_two)
    mixture_grad = jnp.einsum(
        "td,ed->te", middle_grad.astype(jnp.bfloat16), output_w, preferred_element_type=jnp.float32
    ).astype(jnp.bfloat16)
    mixture_grad = mixture_grad.reshape(length, head_count, HEAD)
    scores = attend_scores(queries, keys_all, visible, score_scale)
    attention = jnp.exp(scores - log_total)
    attention_grad = jnp.einsum(
        "qhe,khe->hqk", mixture_grad, values_all, preferred_element_type=jnp.float32
    )
    score_grad = attention * (
        attention_grad - jnp.sum(attention * attention_grad, axis=-1, keepdims=True)
    )
    score_low = score_grad.astype(jnp.bfloat16)
    query_grad = (
        jnp.einsum("hqk,khe->qhe", score_low, keys_all, preferred_element_type=jnp.float32)
        * score_scale
    )
    keys_grad = (
        jnp.einsum("hqk,qhe->khe", score_low, queries, preferred_element_type=jnp.float32)
        * score_scale
    )
    values_grad = jnp.einsum(
        "hqk,qhe->khe",
        attention.astype(jnp.bfloat16),
        mixture_grad,
        preferred_element_type=jnp.float32,
    )
    pair_grad = jnp.concatenate(
        [
            keys_grad[:prefix].reshape(prefix, model_width),
            values_grad[:prefix].reshape(prefix, model_width),
        ],
        axis=1,
    )
    triple_grad = jnp.concatenate(
        [
            query_grad.reshape(length, model_width),
            keys_grad[prefix:].reshape(length, model_width),
            values_grad[prefix:].reshape(length, model_width),
        ],
        axis=1,
    ).astype(jnp.bfloat16)
    first_grad = jnp.einsum("te,de->td", triple_grad, triple_w, preferred_element_type=jnp.float32)
    return (middle_grad + norm_back(first_grad, unit_one, scale_one, gain_one), pair_grad)


def reparam_back(pair_grad, prefix_table, hidden, hidden_low, inner_weight, outer_weight):
    outer_w_grad = jnp.dot(hidden_low.astype(jnp.float32).T, pair_grad, precision=HIGHEST)
    outer_b_grad = jnp.sum(pair_grad, axis=0)
    hidden_grad = jnp.dot(pair_grad, outer_weight.astype(jnp.float32).T, precision=HIGHEST)
    before_grad = hidden_grad * (1.0 - hidden * hidden)
    inner_b_grad = jnp.sum(before_grad, axis=0)
    inner_w_grad = jnp.dot(prefix_table.astype(jnp.float32).T, before_grad, precision=HIGHEST)
    table_grad = jnp.dot(before_grad, inner_weight.astype(jnp.float32).T, precision=HIGHEST)
    return (table_grad, inner_w_grad, inner_b_grad, outer_w_grad, outer_b_grad)


def body(
    activations,
    lengths,
    cotangent,
    gain_first,
    shift_first,
    triple_weight,
    output_weight,
    output_bias,
    gain_second,
    shift_second,
    upward_weight,
    upward_bias,
    downward_weight,
    downward_bias,
    prefix_table,
    inner_weight,
    inner_bias,
    outer_weight,
    outer_bias,
):
    smalls = (
        gain_first,
        shift_first,
        output_bias,
        gain_second,
        shift_second,
        upward_bias,
        downward_bias,
    )
    score_scale = HEAD ** (-0.5)
    length = activations.shape[1]
    model_width = activations.shape[2]
    head_count = model_width // HEAD
    hidden = jnp.tanh(
        jnp.dot(prefix_table, inner_weight, preferred_element_type=jnp.float32) + inner_bias
    )
    hidden_low = hidden.astype(jnp.bfloat16)
    prefix_pairs = (
        jnp.dot(hidden_low, outer_weight, preferred_element_type=jnp.float32) + outer_bias
    ).astype(jnp.bfloat16)
    prefix = prefix_pairs.shape[0]
    prefix_pair = (
        prefix_pairs[:, :model_width].reshape(prefix, head_count, HEAD),
        prefix_pairs[:, model_width:].reshape(prefix, head_count, HEAD),
    )
    pair_total = jnp.zeros((prefix, 2 * model_width), jnp.float32)
    results = []
    input_grads = []
    for micro_index in range(activations.shape[0]):
        weights = collect(triple_weight, output_weight, upward_weight, downward_weight)
        visible = visibility(lengths[micro_index], length, prefix)
        result, saved_state = forward_row(
            activations[micro_index], visible, prefix_pair, weights, smalls, score_scale
        )
        input_grad, pair_grad = backward_row(
            cotangent[micro_index].astype(jnp.float32),
            saved_state,
            visible,
            weights,
            smalls,
            score_scale,
            prefix,
        )
        results.append(result.astype(jnp.bfloat16))
        input_grads.append(input_grad.astype(jnp.bfloat16))
        pair_total = pair_total + pair_grad
    local_grads = reparam_back(
        pair_total, prefix_table, hidden, hidden_low, inner_weight, outer_weight
    )
    gradients = lax.psum(
        (local_grads[0], local_grads[1], local_grads[2], local_grads[3], local_grads[4]),
        ("dp", "fsdp"),
    )
    return (
        jnp.stack(results),
        jnp.stack(input_grads),
        gradients[0],
        gradients[1],
        gradients[2],
        gradients[3],
        gradients[4],
    )


def solution(mesh):
    in_specs = (
        P(("dp", "fsdp"), None, None),
        P(("dp", "fsdp"), None),
        P(("dp", "fsdp"), None, None),
        P(),
        P(),
        P("fsdp", "dp"),
        P("fsdp", "dp"),
        P(),
        P(),
        P(),
        P("fsdp", "dp"),
        P(),
        P("fsdp", "dp"),
        P(),
        P(),
        P(),
        P(),
        P(),
        P(),
    )
    out_specs = (
        P(("dp", "fsdp"), None, None),
        P(("dp", "fsdp"), None, None),
        P(),
        P(),
        P(),
        P(),
        P(),
    )
    return jax.shard_map(body, mesh=mesh, in_specs=in_specs, out_specs=out_specs, check_vma=False)
```

profile of v0, /device:TPU:0, one launch (start us, length us, event | category | flops | bytes accessed | tf_op | source)
XLA Modules:
  0.0 824.8 jit_solution(6865797603766382058)
XLA Ops:
  9.5 28.9 %all-gather.8.cloned.1.call-done = bf16[1024,768]{1,0:T(8,128)(2,1)} async-done(((bf16[128,768]{1,0:T(8,128)(2,1)}), bf16[1024,768]{1,0:T(8,128)(2,1)}) %all-gather.8.cloned.1.call-update) | async-done | bytes 1572880 | tf_op jit(solution)/shard_map/all_gather | solution.py:17
  38.4 10.8 %all_gather.34 = bf16[1024,256]{1,0:T(8,128)(2,1)} all-gather(bf16[128,256]{1,0:T(8,128)(2,1)} %param.25), channel_id=1, replica_groups=mesh['dp'=4,'fsdp'=8] {'fsdp'}, dimensions={0}, use_global_device_ids=true | all-gather | bytes 589824 | tf_op jit(solution)/shard_map/all_gather | solution.py:18
  49.3 18.9 %all-gather.14.cloned.1.call-done = bf16[1024,1024]{1,0:T(8,128)(2,1)} async-done(((bf16[128,1024]{1,0:T(8,128)(2,1)}), bf16[1024,1024]{1,0:T(8,128)(2,1)}) %all-gather.14.cloned.1.call-update) | async-done | bytes 2097168 | tf_op jit(solution)/shard_map/all_gather | solution.py:19
  68.2 29.8 %all-gather.18.cloned.1.call-done = bf16[4096,256]{1,0:T(8,128)(2,1)} async-done(((bf16[512,256]{1,0:T(8,128)(2,1)}), bf16[4096,256]{1,0:T(8,128)(2,1)}) %all-gather.18.cloned.1.call-update) | async-done | bytes 2097168 | tf_op jit(solution)/shard_map/all_gather | solution.py:20
  105.7 109.1 %all-gather.10.cloned.1.call-done = bf16[1024,3072]{1,0:T(8,128)(2,1)} async-done(((bf16[1024,768]{1,0:T(8,128)(2,1)}), bf16[1024,3072]{1,0:T(8,128)(2,1)}) %all-gather.10.cloned.1.call-update) | async-done | bytes 6291472 | tf_op jit(solution)/shard_map/all_gather | solution.py:23
  214.8 4.7 convolution_convert_fusion
  226.9 4.7 convolution_convert_fusion.1
  245.9 14.8 %all-gather.12.cloned.1.call-done = bf16[1024,1024]{1,0:T(8,128)(2,1)} async-done(((bf16[1024,256]{1,0:T(8,128)(2,1)}), bf16[1024,1024]{1,0:T(8,128)(2,1)}) %all-gather.12.cloned.1.call-update) | async-done | bytes 2097168 | tf_op jit(solution)/shard_map/all_gather | solution.py:24
  273.2 136.8 %all-gather.16.cloned.1.call-done = bf16[1024,4096]{1,0:T(8,128)(2,1)} async-done(((bf16[1024,1024]{1,0:T(8,128)(2,1)}), bf16[1024,4096]{1,0:T(8,128)(2,1)}) %all-gather.16.cloned.1.call-update) | async-done | bytes 8388624 | tf_op jit(solution)/shard_map/all_gather | solution.py:25
  410.0 8.2 convolution_add_fusion.1
  418.2 140.7 %all-gather.20.cloned.1.call-done = bf16[4096,1024]{1,0:T(8,128)(2,1)} async-done(((bf16[4096,256]{1,0:T(8,128)(2,1)}), bf16[4096,1024]{1,0:T(8,128)(2,1)}) %all-gather.20.cloned.1.call-update) | async-done | bytes 8388624 | tf_op jit(solution)/shard_map/all_gather | solution.py:26
  558.9 12.6 %fusion.191 = (f32[256]{0:T(256)S(1)}, f32[256]{0:T(256)S(1)}, f32[256,1024]{1,0:T(8,128)}) fusion(f32[256]{0:T(256)S(1)} %add_rsqrt_fusion.2, f32[256,1024]{1,0:T(8,128)} %copy-done.4, f32[256]{0:T(256)S(1)} %broadcast_multiply_fusion.10, f32[1024]{0:T(1024)S(1)} %copy-done.67, bf16[1024,4096]{1,0:T(8,128)(2,1)} %all-gather.16.cloned.1.call-done, ...), kind=kOutput, calls=%fused_computation.251 | convolution fusion | flops 4317511680 | bytes 23601152 | tf_op jit(solution)/shard_map/tf,df->td/dot_general | solution.py:126
  572.1 4.1 convolution_convert_fusion.5
  578.4 3.6 convolution_bitcast_fusion.2
  591.3 5.8 convolution_add_fusion
  597.0 22.8 %fusion.192 = (f32[256]{0:T(256)S(1)}, f32[256]{0:T(256)S(1)}, f32[256,1024]{1,0:T(8,128)}) fusion(f32[256]{0:T(256)S(1)} %copy-done.51, f32[256,1024]{1,0:T(8,128)} %get-tuple-element.65, f32[256]{0:T(256)S(1)} %broadcast_multiply_fusion.8, f32[1024]{0:T(1024)S(1)} %copy-done.68, bf16[1024,4096]{1,0:T(8,128)(2,1)} %all-gather.16.cloned.1.call-done, ...), kind=kOutput, calls=%fused_computation.252 | convolution fusion | flops 4317511680 | bytes 23601152 | tf_op jit(solution)/shard_map/tf,df->td/dot_general | solution.py:126
  619.8 4.1 convolution_convert_fusion.4
  626.0 3.7 convolution_bitcast_fusion.1
  650.7 3.8 fusion.148
  655.2 41.2 %all-reduce.2 = (f32[10,1024]{1,0:T(8,128)}, f32[512]{0:T(512)}, f32[2048]{0:T(1024)}) all-reduce(f32[10,1024]{1,0:T(8,128)S(1)} %fusion.203, f32[512]{0:T(512)S(1)} %copy-done.46, f32[2048]{0:T(1024)S(1)} %fusion.189), channel_id=1, replica_groups=mesh['dp'=4,'fsdp'=8] {'dp','fsdp'}, use_global_device_ids=true, to_apply=%region_26.27 | all-reduce | flops 12800 | bytes 102400 | tf_op jit(solution)/shard_map/psum | solution.py:255
  696.4 8.0 fusion.79
  704.5 6.6 fusion.80
  720.7 89.3 %all-reduce.6.cloned.1.call-done = (f32[1024,512]{0,1:T(8,128)}, f32[512,2048]{1,0:T(8,128)}) async-done(((f32[1024,512]{0,1:T(8,128)}, f32[512,2048]{1,0:T(8,128)}), (f32[1024,512]{0,1:T(8,128)}, f32[512,2048]{1,0:T(8,128)})) %all-reduce.6.cloned.1.call-update) | async-done | bytes 6291472 | tf_op jit(solution)/shard_map/psum | solution.py:255
  812.8 4.7 copy.94
  (268 shorter events, 91.6 us)
Async XLA Ops:
  7.2 93.9 %copy-start = (bf16[512,2048]{1,0:T(8,128)(2,1)S(1)}, bf16[512,2048]{1,0:T(8,128)(2,1)}, u32[]{:S(2)}) copy-start(bf16[512,2048]{1,0:T(8,128)(2,1)} %param.36) | copy-start | bytes 6291460
  7.2 90.9 %copy-start.62 = (s32[2,4]{1,0:T(2,128)S(1)}, s32[2,4]{1,0:T(2,128)}, u32[]{:S(2)}) copy-start(s32[2,4]{1,0:T(2,128)} %param.20) | copy-start | bytes 100
  7.2 91.8 %copy-start.38 = (bf16[10,1024]{1,0:T(8,128)(2,1)S(1)}, bf16[10,1024]{1,0:T(8,128)(2,1)}, u32[]{:S(2)}) copy-start(bf16[10,1024]{1,0:T(8,128)(2,1)} %param.33) | copy-start | bytes 61444
  7.2 91.8 %copy-start.61 = (f32[512]{0:T(512)S(1)}, f32[512]{0:T(512)}, u32[]{:S(2)}) copy-start(f32[512]{0:T(512)} %param.35) | copy-start | bytes 6148
  7.2 31.1 %all-gather.8.cloned.1.call-start = ((), (), s32[]{:S(2)}) async-start(), calls=%async_computation | async-start | bytes 1769472 | tf_op jit(solution)/shard_map/all_gather | solution.py:17
  7.9 60.2 %all-gather.14.cloned.1.call-start = ((), (), s32[]{:S(2)}) async-start(), calls=%async_computation.3 | async-start | bytes 2359296 | tf_op jit(solution)/shard_map/all_gather | solution.py:19
  8.7 89.3 %all-gather.18.cloned.1.call-start = ((), (), s32[]{:S(2)}) async-start(), calls=%async_computation.5 | async-start | bytes 2359296 | tf_op jit(solution)/shard_map/all_gather | solution.py:20
  9.4 205.4 %all-gather.10.cloned.1.call-start = ((), (), s32[]{:S(2)}) async-start(), calls=%async_computation.1 | async-start | bytes 7864320 | tf_op jit(solution)/shard_map/all_gather | solution.py:23
  38.4 62.7 %copy-start.45 = (f32[2048]{0:T(1024)S(1)}, f32[2048]{0:T(1024)}, u32[]{:S(2)}) copy-start(f32[2048]{0:T(1024)} %param.37) | copy-start | bytes 24580
  38.4 222.3 %all-gather.12.cloned.1.call-start = ((), (), s32[]{:S(2)}) async-start(), calls=%async_computation.2 | async-start | bytes 2621440 | tf_op jit(solution)/shard_map/all_gather | solution.py:24
  49.2 360.8 %all-gather.16.cloned.1.call-start = ((), (), s32[]{:S(2)}) async-start(), calls=%async_computation.4 | async-start | bytes 10485760 | tf_op jit(solution)/shard_map/all_gather | solution.py:25
  68.2 35.7 %copy-start.3 = (bf16[2,256,1024]{2,1,0:T(8,128)(2,1)S(1)}, bf16[2,256,1024]{2,1,0:T(8,128)(2,1)}, u32[]{:S(2)}) copy-start(bf16[2,256,1024]{2,1,0:T(8,128)(2,1)} %param.19) | copy-start | bytes 3145732
  68.2 490.7 %all-gather.20.cloned.1.call-start = ((), (), s32[]{:S(2)}) async-start(), calls=%async_computation.6 | async-start | bytes 10485760 | tf_op jit(solution)/shard_map/all_gather | solution.py:26
  98.0 711.9 %all-reduce.6.cloned.1.call-start = ((), (), s32[]{:S(2)}) async-start(), calls=%async_computation.7 | async-start | bytes 12582912 | tf_op jit(solution)/shard_map/psum | solution.py:255
  103.9 163.0 %copy-start.9 = (bf16[10,1024]{0,1:T(8,128)(2,1)}, bf16[10,1024]{0,1:T(8,128)(2,1)S(1)}, u32[]{:S(2)}) copy-start(bf16[10,1024]{0,1:T(8,128)(2,1)S(1)} %copy.90) | copy-start | bytes 61444
  104.2 115.4 %copy-start.43 = (f32[256]{0:T(256)}, f32[256]{0:T(256)S(1)}, u32[]{:S(2)}) copy-start(f32[256]{0:T(256)S(1)} %get-tuple-element.79) | copy-start | bytes 3076
  104.2 122.8 %copy-start.41 = (f32[256]{0:T(256)}, f32[256]{0:T(256)S(1)}, u32[]{:S(2)}) copy-start(f32[256]{0:T(256)S(1)} %get-tuple-element.80) | copy-start | bytes 3076
  242.5 18.2 %copy-start.40 = (f32[1024]{0:T(1024)S(1)}, f32[1024]{0:T(1024)}, u32[]{:S(2)}) copy-start(f32[1024]{0:T(1024)} %param.26) | copy-start | bytes 12292
  268.4 141.6 %copy-start.63 = (f32[4096]{0:T(1024)S(1)}, f32[4096]{0:T(1024)}, u32[]{:S(2)}) copy-start(f32[4096]{0:T(1024)} %param.30) | copy-start | bytes 49156
  268.4 141.6 %copy-start.65 = (f32[1024]{0:T(1024)S(1)}, f32[1024]{0:T(1024)}, u32[]{:S(2)}) copy-start(f32[1024]{0:T(1024)} %param.28) | copy-start | bytes 12292
  268.4 141.6 %copy-start.67 = (f32[1024]{0:T(1024)S(1)}, f32[1024]{0:T(1024)}, u32[]{:S(2)}) copy-start(f32[1024]{0:T(1024)} %param.27) | copy-start | bytes 12292
  272.7 286.2 %copy-start.49 = (f32[256]{0:T(256)}, f32[256]{0:T(256)S(1)}, u32[]{:S(2)}) copy-start(f32[256]{0:T(256)S(1)} %add_rsqrt_fusion.2) | copy-start | bytes 3076
  654.5 41.9 %copy-start.69 = (f32[1024]{0:T(1024)S(1)}, f32[1024]{0:T(1024)}, u32[]{:S(2)}) copy-start(f32[1024]{0:T(1024)} %param.32) | copy-start | bytes 12292
  696.4 15.8 %slice-start.6 = ((s8[6291456]{0:T(1024)(128)(4,1)}), s8[4194304]{0:T(1024)(128)(4,1)S(1)}, s32[]{:S(2)}) async-start(s8[6291456]{0:T(1024)(128)(4,1)} %bitcast.232), calls=%async_computation.14 | async-start | bytes 8388608
  (66 other events, 278.1 us)
Sparse Core Ops, SparseCore 0:
  9.9 28.3 all-gather.7
  40.2 27.8 all-gather.13
  70.1 27.8 all-gather.17
  99.4 115.3 all-gather.9
  216.2 44.4 all-gather.11
  262.1 147.8 all-gather.15
  411.6 147.3 all-gather.19
  654.6 155.2 all-reduce.5
where the time goes:
time: 835 us; the launch traced here: 825 us
  waiting for transfers between devices  570 us (68%)
  matrix products  126 us (15%)
  blocking collectives  52 us (6%)
  local copies, waits for them, and re-layouts  46.5 us (6%)
  between operations  15.7 us (2%)
  other arithmetic  14.4 us (2%)
    all_gather x1, waiting for transfers between devices, collect(): lax.all_gather(by_rows[3], 'dp', axis=1, tiled=True)  141 us
    all_gather x1, waiting for transfers between devices, collect(): lax.all_gather(by_rows[2], 'dp', axis=1, tiled=True)  137 us
    all_gather x1, waiting for transfers between devices, collect(): lax.all_gather(by_rows[0], 'dp', axis=1, tiled=True)  109 us
    psum x1, waiting for transfers between devices, body(): lax.psum((local_grads[0], local_grads[1], local_grads[2], local_grads[3],...  89.3 us
    psum x1, blocking collectives, body(): lax.psum((local_grads[0], local_grads[1], local_grads[2], local_grads[3],...  41.2 us
    dot_general x2, matrix products, backward_row(): jnp.einsum('tf,df->td', upward_grad, upward_w, preferred_element_type=jnp...  35.4 us
    all_gather x1, waiting for transfers between devices, collect(): lax.all_gather(downward_weight, 'fsdp', axis=0, tiled=True)  29.8 us
    all_gather x1, waiting for transfers between devices, collect(): lax.all_gather(triple_weight, 'fsdp', axis=0, tiled=True)  28.9 us
  transfers between devices with their start and end apart: 8, of which 8 were waited for; matrix products, arithmetic and copies ran while one was open for 10% of the time, Pallas kernels for 0%

commit v1 on v0

v1 whole, which is shorter than its diff:
```python
from functools import partial

import jax
import jax.numpy as jnp
from jax import lax
from jax.experimental import pallas as pl
from jax.experimental.pallas import tpu as pltpu
from jax.sharding import PartitionSpec as P

HEAD = 64
PAD = 16
MASKED = -1e30
F32 = jnp.float32
BF16 = jnp.bfloat16
GELU_C = 0.7978845608028654
GELU_A = 0.044715

ANY = pl.BlockSpec(memory_space=pl.ANY)
VMEM = pl.BlockSpec(memory_space=pltpu.VMEM)
SMEM = pl.BlockSpec(memory_space=pltpu.SMEM)


def dot(a, b):
    return lax.dot_general(a, b, (((1,), (0,)), ((), ())), preferred_element_type=F32)


def dot_nt(a, b):
    return lax.dot_general(a, b, (((1,), (1,)), ((), ())), preferred_element_type=F32)


def dot_tn(a, b):
    return lax.dot_general(a, b, (((0,), (0,)), ((), ())), preferred_element_type=F32)


def unit(values):
    center = values - jnp.mean(values, axis=-1, keepdims=True)
    scaled = lax.rsqrt(jnp.mean(center * center, axis=-1, keepdims=True) + 1e-05)
    return center * scaled, scaled


def norm_back(upstream, unit_rows, scaled):
    return scaled * (
        upstream
        - jnp.mean(upstream, axis=-1, keepdims=True)
        - unit_rows * jnp.mean(upstream * unit_rows, axis=-1, keepdims=True)
    )


def call(body, name, outs, ins, scratch, flops, bytes_accessed, vmem=56):
    return pl.pallas_call(
        body,
        name=name,
        out_shape=[o[0] for o in outs],
        out_specs=[o[1] for o in outs],
        in_specs=ins,
        scratch_shapes=scratch,
        compiler_params=pltpu.CompilerParams(vmem_limit_bytes=vmem * 1024 * 1024),
        cost_estimate=pl.CostEstimate(
            flops=flops, bytes_accessed=bytes_accessed, transcendentals=0
        ),
    )


def shaped(shape, dtype):
    return jax.ShapeDtypeStruct(shape, dtype)


class Pieces:
    def __init__(self, fsdp, dp, shard_rows, shard_cols):
        self.fsdp, self.dp = fsdp, dp
        self.shard_rows, self.shard_cols = shard_rows, shard_cols
        self.parts = []

    def whole(self, key):
        self.parts.append((key, None, None, None, None, None, None))
        return self

    def add(self, key, first, count, flip, planes, col):
        rows = self.shard_rows
        for k, plane in enumerate(planes):
            low, high = max(first, k * rows), min(first + count, (k + 1) * rows)
            if low < high:
                self.parts.append((key, low - first, high - low, flip, plane, low - k * rows, col))

    def copies(self, refs, dst, sems, base, place, only=None):
        out = []
        for key, src_row, count, flip, plane, shard_row, col in self.parts:
            if flip is None:
                out.append(pltpu.make_async_copy(refs[key], dst, sems.at[base + len(out)]))
                continue
            if only is not None and flip >> 1 != only:
                continue
            owner = jnp.bitwise_xor(place[1], flip)
            if only is not None:
                owner = jnp.bitwise_and(owner, 1)
            row = pl.multiple_of(owner * self.shard_rows + shard_row, 16)
            across = lax.rem(place[0] + plane, self.dp)
            column = pl.multiple_of(across * self.shard_cols, 128)
            out.append(
                pltpu.make_async_copy(
                    refs[key].at[pl.ds(src_row, count), pl.ds(col, self.shard_cols)],
                    dst.at[pl.ds(row, count), pl.ds(column, self.shard_cols)],
                    sems.at[base + len(out)],
                )
            )
        return out


def start(copies):
    for c in copies:
        c.start()


def wait(copies):
    for c in copies:
        c.wait()


def flip(value, mask, size):
    return lax.ppermute(value, "fsdp", [(i, i ^ mask) for i in range(size)])


def spread(stack, size):
    half = stack.shape[0] // 2
    along_x = flip(stack, 2, size)
    along_y = flip(stack, 4, size)
    diag_x = flip(along_y[:half], 2, size)
    diag_y = flip(along_x[half:], 4, size)
    lane = [stack, along_x, along_y, diag_x, diag_y]
    return lane + [flip(a, 1, size) for a in lane]


def add_spread(pieces, keys, planes, col):
    total = pieces.shard_rows * len(planes)
    half = total // 2
    for core in (0, 1):
        own, along_x, along_y, diag_x, diag_y = keys[5 * core : 5 * core + 5]
        pieces.add(own, 0, total, core, planes, col)
        pieces.add(along_x, 0, total, 2 | core, planes, col)
        pieces.add(along_y, 0, total, 4 | core, planes, col)
        pieces.add(diag_x, 0, half, 6 | core, planes, col)
        pieces.add(diag_y, half, total - half, 6 | core, planes, col)


def foreign(value, dp, place_z):
    planes = lax.all_gather(value, "dp", axis=0, tiled=False)
    rows = [
        lax.dynamic_index_in_dim(planes, lax.rem(place_z + j, dp), 0, keepdims=False)
        for j in range(1, dp)
    ]
    return jnp.concatenate(rows, axis=0)


def collect(triple_w, output_w, upward_w, downward_w, fsdp, dp):
    if fsdp != 8 or dp < 2:
        out = []
        for w in (triple_w, output_w, upward_w, downward_w):
            rows = lax.all_gather(w, "fsdp", axis=0, tiled=True)
            full = lax.all_gather(rows, "dp", axis=1, tiled=True)
            pieces = Pieces(fsdp, dp, w.shape[0], w.shape[1]).whole(0)
            out.append(([full], pieces))
        (t, tp), (o, op), u, d = out
        op = Pieces(fsdp, dp, output_w.shape[0], output_w.shape[1]).whole(1)
        return ([t[0], o[0]], tp, op), u, d
    place_z = lax.axis_index("dp")
    triple_c, output_c, upward_c = (w.shape[1] for w in (triple_w, output_w, upward_w))
    first = jnp.concatenate([triple_w, output_w], axis=1)
    first_far = foreign(first, dp, place_z)
    upward_far = foreign(upward_w, dp, place_z)
    downward_far = foreign(downward_w, dp, place_z)
    near = jnp.concatenate([triple_w, output_w, upward_w], axis=1)
    near_all = spread(near, fsdp)
    down_near = spread(downward_w, fsdp)
    first_all = spread(first_far, fsdp)
    upward_all = spread(upward_far, fsdp)
    downward_all = spread(downward_far, fsdp)
    far = list(range(1, dp))

    def pieces(w, near_col, far_col):
        p = Pieces(fsdp, dp, w.shape[0], w.shape[1])
        add_spread(p, list(range(10)), [0], near_col)
        add_spread(p, list(range(10, 20)), far, far_col)
        return p

    return (
        (near_all + first_all, pieces(triple_w, 0, 0), pieces(output_w, triple_c, triple_c)),
        (near_all + upward_all, pieces(upward_w, triple_c + output_c, 0)),
        (down_near + downward_all, pieces(downward_w, 0, 0)),
    )


def prefix_body(prefix, table, inner_w, inner_b, outer_w, outer_b, hidden_o, keys_o, values_o, ones_o):
    width = keys_o.shape[1]
    hidden = jnp.tanh(dot(table[...], inner_w[...]) + inner_b[...])
    hidden_o[...] = hidden
    pairs = (dot(hidden.astype(BF16), outer_w[...]) + outer_b[...]).astype(BF16).astype(F32)
    shape = keys_o.shape
    row = lax.broadcasted_iota(jnp.int32, shape, 0)
    col = lax.broadcasted_iota(jnp.int32, shape, 1)
    inside = (row // PAD) == (col // HEAD)
    real = inside & (lax.rem(row, PAD) < prefix)
    heads = shape[0] // PAD
    keys_o[...] = jnp.where(real, jnp.tile(pairs[:, :width], (heads, 1)), 0.0).astype(BF16)
    values_o[...] = jnp.where(real, jnp.tile(pairs[:, width:], (heads, 1)), 0.0).astype(BF16)
    ones_o[...] = jnp.where(inside, 1.0, 0.0).astype(BF16)


def attend_body(rows, prefix, parts_t, parts_o, n_arrays, *refs):
    place, lengths, x, gain1, shift1, out_b, gain2, shift2, bdk, bdv = refs[:10]
    arrays = refs[10 : 10 + n_arrays]
    triple_o, prob_o, pre_o, mix_o, middle_o, norm_o, t_o, o_o = refs[10 + n_arrays : 18 + n_arrays]
    (tv, ov, normed, tri, prob, bias, spre, pre, main, mix, middle, sems, out_sems) = refs[
        18 + n_arrays :
    ]
    tokens, width = x.shape
    length = tokens // rows
    heads = width // HEAD
    scale = HEAD ** (-0.5)
    in_t = parts_t.copies(arrays, tv, sems, 0, place)
    in_o = parts_o.copies(arrays, ov, sems, len(in_t), place)
    start(in_t)
    start(in_o)
    step = 128
    for t in range(0, tokens, step):
        u, _ = unit(x[t : t + step, :].astype(F32))
        normed[t : t + step, :] = (u * gain1[...] + shift1[...]).astype(BF16)
    wait(in_t)
    outs = [pltpu.make_async_copy(tv, t_o, out_sems.at[0])]
    outs[0].start()

    def triple_block(n, carry):
        cols = pl.ds(pl.multiple_of(n * 512, 512), 512)
        tri[:, cols] = dot(normed[...], tv[:, cols]).astype(BF16)
        return carry

    lax.fori_loop(0, 3 * width // 512, triple_block, 0)
    outs.append(pltpu.make_async_copy(tri, triple_o, out_sems.at[1]))
    outs[1].start()

    lane = lax.broadcasted_iota(jnp.int32, (length, 2 * HEAD), 1)
    low_lane = lane < HEAD
    for row in range(rows):
        here = slice(row * length, (row + 1) * length)
        key = lax.broadcasted_iota(jnp.int32, (length, length), 0)
        query = lax.broadcasted_iota(jnp.int32, (length, length), 1)
        key_seg = jnp.zeros((length, length), jnp.int32)
        query_seg = jnp.zeros((length, length), jnp.int32)
        bound = 0
        for s in range(lengths.shape[1]):
            bound = bound + lengths[row, s]
            key_seg = key_seg + jnp.where(key >= bound, 1, 0)
            query_seg = query_seg + jnp.where(query >= bound, 1, 0)
        seen = (key_seg == query_seg) & (key <= query)
        bias[...] = jnp.where(seen, 0.0, MASKED)
        raw = dot_nt(bdk[...], tri[here, :width]) * scale
        pre_row = lax.broadcasted_iota(jnp.int32, raw.shape, 0)
        spre[...] = jnp.where(lax.rem(pre_row, PAD) < prefix, raw, MASKED)

        def pair(i, carry):
            cols = pl.multiple_of(i * 2 * HEAD, 2 * HEAD)
            q = tri[here, pl.ds(cols, 2 * HEAD)]
            k = tri[here, pl.ds(pl.multiple_of(width + cols, 2 * HEAD), 2 * HEAD)]
            v = tri[here, pl.ds(pl.multiple_of(2 * width + cols, 2 * HEAD), 2 * HEAD)]
            vt = v.T
            found = []
            for sub in (0, 1):
                qm = jnp.where(low_lane if sub == 0 else ~low_lane, q, jnp.zeros_like(q))
                s = dot_nt(k, qm) * scale + bias[...]
                at = pl.multiple_of((2 * i + sub) * PAD, PAD)
                sp = spre[pl.ds(at, PAD), :]
                top = jnp.maximum(
                    jnp.max(s, axis=0, keepdims=True), jnp.max(sp, axis=0, keepdims=True)
                )
                e = jnp.exp(s - top)
                ep = jnp.exp(sp - top)
                inverse = 1.0 / (
                    jnp.sum(e, axis=0, keepdims=True) + jnp.sum(ep, axis=0, keepdims=True)
                )
                p = (e * inverse).astype(BF16)
                prob[row * heads + 2 * i + sub] = p
                pre[row, pl.ds(at, PAD), :] = (ep * inverse).astype(BF16)
                found.append(dot(vt[sub * HEAD : (sub + 1) * HEAD, :], p))
            main[:, pl.ds(cols, 2 * HEAD)] = jnp.concatenate(found, axis=0).T
            return carry

        lax.fori_loop(0, heads // 2, pair, 0)
        outs.append(
            pltpu.make_async_copy(
                prob.at[pl.ds(row * heads, heads)],
                prob_o.at[pl.ds(row * heads, heads)],
                out_sems.at[len(outs)],
            )
        )
        outs[-1].start()
        mix[here, :] = (main[...] + dot_tn(pre[row], bdv[...])).astype(BF16)

    outs.append(pltpu.make_async_copy(pre, pre_o, out_sems.at[len(outs)]))
    outs[-1].start()
    outs.append(pltpu.make_async_copy(mix, mix_o, out_sems.at[len(outs)]))
    outs[-1].start()
    wait(in_o)
    outs.append(pltpu.make_async_copy(ov, o_o, out_sems.at[len(outs)]))
    outs[-1].start()

    def project(n, carry):
        cols = pl.ds(pl.multiple_of(n * 512, 512), 512)
        middle[:, cols] = (
            x[:, cols].astype(F32) + dot(mix[...], ov[:, cols]) + out_b[:, cols]
        )
        return carry

    lax.fori_loop(0, width // 512, project, 0)
    outs.append(pltpu.make_async_copy(middle, middle_o, out_sems.at[len(outs)]))
    outs[-1].start()
    for t in range(0, tokens, step):
        u, _ = unit(middle[t : t + step, :])
        normed[t : t + step, :] = (u * gain2[...] + shift2[...]).astype(BF16)
    outs.append(pltpu.make_async_copy(normed, norm_o, out_sems.at[len(outs)]))
    outs[-1].start()
    wait(outs)


def upward_body(parts, n_arrays, *refs):
    place, norm, bias = refs[:3]
    arrays = refs[3 : 3 + n_arrays]
    active_o, slope_o, up_o = refs[3 + n_arrays : 6 + n_arrays]
    uv, active, slope, sems, out_sems = refs[6 + n_arrays :]
    inward = parts.copies(arrays, uv, sems, 0, place)
    start(inward)
    wait(inward)
    out = pltpu.make_async_copy(uv, up_o, out_sems.at[0])
    out.start()
    block = 512

    def step(n, carry):
        cols = pl.ds(pl.multiple_of(n * block, block), block)
        u = dot(norm[...], uv[:, cols]) + bias[:, cols]
        square = u * u
        t = jnp.tanh(GELU_C * u * (1.0 + GELU_A * square))
        half = 0.5 * (1.0 + t)
        active[:, cols] = (u * half).astype(BF16)
        slope[:, cols] = (
            half + 0.5 * u * (1.0 - t * t) * (GELU_C + 3.0 * GELU_C * GELU_A * square)
        ).astype(BF16)
        return carry

    lax.fori_loop(0, uv.shape[1] // block, step, 0)
    done = [
        pltpu.make_async_copy(active, active_o, out_sems.at[1]),
        pltpu.make_async_copy(slope, slope_o, out_sems.at[2]),
    ]
    start(done)
    out.wait()
    wait(done)


def chunk_start(place, pick, parts, arrays, full, dv, uc, ac, sc, sems, base):
    active, slope, upward = full
    size = uc.shape[1]
    chunk = jnp.bitwise_xor(lax.shift_right_logical(place[1], 1), pick)
    cols = pl.ds(pl.multiple_of(chunk * size, size), size)
    if parts.parts[0][3] is None:
        down = [
            pltpu.make_async_copy(
                arrays[0].at[pl.ds(pl.multiple_of(chunk * size, size), size), :],
                dv,
                sems.at[base],
            )
        ]
    else:
        down = parts.copies(arrays, dv, sems, base, place, only=pick)
    base += len(down)
    rest = [
        pltpu.make_async_copy(slope.at[:, cols], sc, sems.at[base]),
        pltpu.make_async_copy(upward.at[:, cols], uc, sems.at[base + 1]),
        pltpu.make_async_copy(active.at[:, cols], ac, sems.at[base + 2]),
    ]
    start(rest[:1])
    start(down)
    start(rest[1:])
    return down, rest


def chunk_work(g, down, rest, dv, uc, ac, sc, gu, second, out, fresh):
    size = uc.shape[1]
    width = second.shape[1]
    wait(down)
    rest[0].wait()

    def upstream(n, carry):
        cols = pl.ds(pl.multiple_of(n * 512, 512), 512)
        gu[:, cols] = (dot_nt(g[...], dv[cols, :]) * sc[:, cols].astype(F32)).astype(BF16)
        return carry

    lax.fori_loop(0, size // 512, upstream, 0)
    rest[1].wait()

    def back(n, carry):
        cols = pl.ds(pl.multiple_of(n * 512, 512), 512)
        value = dot_nt(gu[...], uc[cols, :])
        second[:, cols] = value if fresh else second[:, cols] + value
        return carry

    lax.fori_loop(0, width // 512, back, 0)
    rest[2].wait()

    def ahead(n, carry):
        cols = pl.ds(pl.multiple_of(n * 512, 512), 512)
        value = dot(ac[...], dv[:, cols])
        out[:, cols] = value if fresh else out[:, cols] + value
        return carry

    lax.fori_loop(0, width // 512, ahead, 0)


def chunk_body(picks, first, parts, n_arrays, *refs):
    place, g, active, slope, upward = refs[:5]
    arrays = refs[5 : 5 + n_arrays]
    rest = refs[5 + n_arrays :]
    if not first:
        second_i, out_i = rest[:2]
        rest = rest[2:]
    second_o, out_o, dv, uc, ac, sc, gu, second, out, sems, io_sems = rest
    if not first:
        carried = [
            pltpu.make_async_copy(second_i, second, io_sems.at[0]),
            pltpu.make_async_copy(out_i, out, io_sems.at[1]),
        ]
        start(carried)
    for k, pick in enumerate(picks):
        down, more = chunk_start(
            place, pick, parts, arrays, (active, slope, upward), dv, uc, ac, sc, sems, 0
        )
        if not first and k == 0:
            wait(carried)
        chunk_work(g, down, more, dv, uc, ac, sc, gu, second, out, first and k == 0)
    done = [
        pltpu.make_async_copy(second, second_o, io_sems.at[2]),
        pltpu.make_async_copy(out, out_o, io_sems.at[3]),
    ]
    start(done)
    wait(done)


def middle_body(rows, picks, parts, n_arrays, *refs):
    place, g, active, slope, upward = refs[:5]
    arrays = refs[5 : 5 + n_arrays]
    second_i, out_i, middle_i, gain2, down_b, output_w, mix, triple, pre, bdv, ones = refs[
        5 + n_arrays : 16 + n_arrays
    ]
    result_o, gmid_o, gmix_o, delta_o, dspre_o, pairs_o = refs[16 + n_arrays : 22 + n_arrays]
    (dv, uc, ac, sc, gu, second, out, middle, ov, low, gmix, q, result, sems, io_sems) = refs[
        22 + n_arrays :
    ]
    tokens, width = g.shape
    length = tokens // rows
    heads = width // HEAD
    scale = HEAD ** (-0.5)
    carried = [
        pltpu.make_async_copy(second_i, second, io_sems.at[0]),
        pltpu.make_async_copy(out_i, out, io_sems.at[1]),
    ]
    later = [
        pltpu.make_async_copy(middle_i, middle, io_sems.at[2]),
        pltpu.make_async_copy(output_w, ov, io_sems.at[3]),
        pltpu.make_async_copy(triple.at[:, pl.ds(0, width)], q, io_sems.at[4]),
    ]
    for k, pick in enumerate(picks):
        down, more = chunk_start(
            place, pick, parts, arrays, (active, slope, upward), dv, uc, ac, sc, sems, 0
        )
        if k == 0:
            start(carried)
            start(later)
            wait(carried)
        chunk_work(g, down, more, dv, uc, ac, sc, gu, second, out, False)
    wait(later)
    step = 128
    for t in range(0, tokens, step):
        here = slice(t, t + step)
        mid = middle[here, :]
        u, scaled = unit(mid)
        gm = g[here, :].astype(F32) + norm_back(second[here, :] * gain2[...], u, scaled)
        second[here, :] = gm
        low[here, :] = gm.astype(BF16)
        result[here, :] = (mid + out[here, :] + down_b[...]).astype(BF16)
    done = [
        pltpu.make_async_copy(second, gmid_o, io_sems.at[5]),
        pltpu.make_async_copy(result, result_o, io_sems.at[6]),
    ]
    start(done)

    def back(n, carry):
        rows_n = pl.ds(pl.multiple_of(n * 512, 512), 512)
        gmix[:, rows_n] = dot_nt(low[...], ov[rows_n, :]).astype(BF16)
        return carry

    lax.fori_loop(0, width // 512, back, 0)
    done.append(pltpu.make_async_copy(gmix, gmix_o, io_sems.at[7]))
    done[-1].start()
    keys = jnp.zeros((heads * PAD, width), F32)
    values = jnp.zeros((heads * PAD, width), F32)
    for row in range(rows):
        here = slice(row * length, (row + 1) * length)
        up = gmix[here, :]
        product = up.astype(F32) * mix[here, :].astype(F32)
        high = product.astype(BF16)
        small = (product - high.astype(F32)).astype(BF16)
        delta = dot_nt(ones[...], high) + dot_nt(ones[...], small)
        delta_o[row] = delta
        p = pre[row]
        ds = (p.astype(F32) * (dot_nt(bdv[...], up) - delta)).astype(BF16)
        dspre_o[row] = ds
        keys = keys + dot(ds, q[here, :])
        values = values + dot(p, up)
    row = lax.broadcasted_iota(jnp.int32, keys.shape, 0)
    col = lax.broadcasted_iota(jnp.int32, keys.shape, 1)
    inside = (row // PAD) == (col // HEAD)
    keys = jnp.where(inside, keys * scale, 0.0).reshape(heads, PAD, width)
    values = jnp.where(inside, values, 0.0).reshape(heads, PAD, width)
    pairs_o[0] = jnp.sum(keys, axis=0)
    pairs_o[1] = jnp.sum(values, axis=0)
    wait(done)


def attend_back_body(row, length, heads, triple, gmix, prob, delta, dspre, bdk, out, tri, up, p, sems):
    width = heads * HEAD
    scale = HEAD ** (-0.5)
    here = pl.ds(row * length, length)
    inward = [
        pltpu.make_async_copy(triple.at[here, :], tri, sems.at[0]),
        pltpu.make_async_copy(gmix.at[here, :], up, sems.at[1]),
        pltpu.make_async_copy(prob.at[pl.ds(row * heads, heads)], p, sems.at[2]),
    ]
    start(inward)
    wait(inward)
    low_lane = lax.broadcasted_iota(jnp.int32, (length, 2 * HEAD), 1) < HEAD
    out[:, :width] = (dot_tn(dspre[row], bdk[...]) * scale).astype(BF16)

    def pair(i, carry):
        cols = pl.multiple_of(i * 2 * HEAD, 2 * HEAD)
        q = tri[:, pl.ds(cols, 2 * HEAD)]
        k = tri[:, pl.ds(pl.multiple_of(width + cols, 2 * HEAD), 2 * HEAD)]
        v = tri[:, pl.ds(pl.multiple_of(2 * width + cols, 2 * HEAD), 2 * HEAD)]
        g = up[:, pl.ds(cols, 2 * HEAD)]
        kt = k.T
        zero = jnp.zeros_like(q)
        queries, keys, values = [], 0.0, 0.0
        for sub in (0, 1):
            side = low_lane if sub == 0 else ~low_lane
            gm = jnp.where(side, g, zero)
            qm = jnp.where(side, q, zero)
            prob_here = p[2 * i + sub]
            at = pl.multiple_of((2 * i + sub) * PAD, PAD)
            d = delta[row, pl.ds(at, PAD), :][:1, :]
            ds = (prob_here.astype(F32) * (dot_nt(v, gm) - d)).astype(BF16)
            queries.append(dot(kt[sub * HEAD : (sub + 1) * HEAD, :], ds))
            keys = keys + dot(ds, qm)
            values = values + dot(prob_here, gm)
        before = dot_tn(dspre[row], bdk[:, pl.ds(cols, 2 * HEAD)])
        dq = jnp.concatenate(queries, axis=0).T + before
        out[:, pl.ds(cols, 2 * HEAD)] = (dq * scale).astype(BF16)
        out[:, pl.ds(pl.multiple_of(width + cols, 2 * HEAD), 2 * HEAD)] = (keys * scale).astype(
            BF16
        )
        out[:, pl.ds(pl.multiple_of(2 * width + cols, 2 * HEAD), 2 * HEAD)] = values.astype(BF16)
        return carry

    lax.fori_loop(0, heads // 2, pair, 0)


def input_body(rows, *refs):
    grads = refs[:rows]
    triple_w, x, gain1, gmid_i, result, tv, first, gmid, sems = refs[rows:]
    tokens, width = x.shape
    length = tokens // rows
    block = 256
    inward = [
        pltpu.make_async_copy(
            triple_w.at[pl.ds(n * block, block), :], tv.at[pl.ds(n * block, block), :], sems.at[n]
        )
        for n in range(width // block)
    ]
    start(inward)
    late = pltpu.make_async_copy(gmid_i, gmid, sems.at[len(inward)])
    late.start()
    for n in range(width // block):
        inward[n].wait()
        for row in range(rows):
            first[row * length : (row + 1) * length, n * block : (n + 1) * block] = dot_nt(
                grads[row][...], tv[n * block : (n + 1) * block, :]
            )
    late.wait()
    step = 128
    for t in range(0, tokens, step):
        here = slice(t, t + step)
        u, scaled = unit(x[here, :].astype(F32))
        back = norm_back(first[here, :] * gain1[...], u, scaled)
        result[here, :] = (gmid[here, :] + back).astype(BF16)


def split3(value):
    high = value.astype(BF16)
    rest = value - high.astype(F32)
    mid = rest.astype(BF16)
    return high, mid, (rest - mid.astype(F32)).astype(BF16)


def reparam_body(prefix, keys, values, hidden_r, table, inner_w, outer_w, *outs):
    table_o, inner_wo, inner_bo, outer_wo, outer_bo = outs
    width = keys.shape[1]
    hidden = hidden_r[...]
    low = hidden.astype(BF16)
    row = lax.broadcasted_iota(jnp.int32, (PAD, hidden.shape[1]), 0)
    grads = []
    for k, ref in enumerate((keys, values)):
        value = ref[...]
        parts = split3(value)
        cols = slice(k * width, (k + 1) * width)
        outer_wo[:, cols] = dot_tn(
            jnp.concatenate([low] * 3, axis=0), jnp.concatenate(parts, axis=0)
        )
        outer_bo[:, cols] = jnp.sum(value, axis=0, keepdims=True)
        grads.append(dot_nt(jnp.concatenate(parts, axis=0), outer_w[:, cols]))
    total = grads[0] + grads[1]
    hidden_grad = total[:PAD] + total[PAD : 2 * PAD] + total[2 * PAD :]
    before = jnp.where(row < prefix, hidden_grad * (1.0 - hidden * hidden), 0.0)
    inner_bo[...] = jnp.sum(before, axis=0, keepdims=True)
    stacked = jnp.concatenate(split3(before), axis=0)
    inner_wo[...] = dot_tn(jnp.concatenate([table[...]] * 3, axis=0), stacked)
    back = dot_nt(stacked, inner_w[...])
    table_o[...] = back[:PAD] + back[PAD : 2 * PAD] + back[2 * PAD :]


def add_over(value, axis, size, first):
    mask = first
    while mask < size:
        value = value + lax.ppermute(value, axis, [(i, i ^ mask) for i in range(size)])
        mask *= 2
    return value


def total_pairs(pairs, fsdp, dp):
    core = lax.rem(lax.axis_index("fsdp"), 2)
    kept = jnp.where(core == 0, pairs[0], pairs[1])
    sent = jnp.where(core == 0, pairs[1], pairs[0])
    value = kept + flip(sent, 1, fsdp)
    value = add_over(value, "fsdp", fsdp, 2)
    value = add_over(value, "dp", dp, 1)
    other = flip(value, 1, fsdp)
    return jnp.where(core == 0, value, other), jnp.where(core == 0, other, value)


def body(
    fsdp,
    dp,
    activations,
    lengths,
    cotangent,
    gain_first,
    shift_first,
    triple_weight,
    output_weight,
    output_bias,
    gain_second,
    shift_second,
    upward_weight,
    upward_bias,
    downward_weight,
    downward_bias,
    prefix_table,
    inner_weight,
    inner_bias,
    outer_weight,
    outer_bias,
):
    rows, length, width = activations.shape
    tokens = rows * length
    heads = width // HEAD
    wide = upward_bias.shape[0]
    prefix, _ = prefix_table.shape
    mid = inner_bias.shape[0]
    chunk = wide // 4
    place = jnp.stack([lax.axis_index("dp"), lax.axis_index("fsdp")]).astype(jnp.int32)
    x = activations.reshape(tokens, width)
    g = cotangent.reshape(tokens, width)
    flat = lambda v: v.reshape(1, -1)
    dma = lambda n: pltpu.SemaphoreType.DMA((n,))
    vm = pltpu.VMEM
    mm = tokens * width * width

    (first_arrays, triple_parts, output_parts), (up_arrays, up_parts), (down_arrays, down_parts) = (
        collect(triple_weight, output_weight, upward_weight, downward_weight, fsdp, dp)
    )

    table = jnp.pad(prefix_table, ((0, PAD - prefix), (0, 0)))
    hidden, bdk, bdv, ones = call(
        partial(prefix_body, prefix),
        "prefix",
        [(shaped((PAD, mid), F32), VMEM)] + [(shaped((heads * PAD, width), BF16), VMEM)] * 3,
        [VMEM] * 5,
        [],
        2 * PAD * mid * 3 * width,
        3 << 20,
    )(table, inner_weight, flat(inner_bias), outer_weight, flat(outer_bias))

    n = len(first_arrays)
    triple, prob, pre, mix, middle, norm_two, triple_full, output_full = call(
        partial(attend_body, rows, prefix, triple_parts, output_parts, n),
        "attend",
        [
            (shaped((tokens, 3 * width), BF16), ANY),
            (shaped((rows * heads, length, length), BF16), ANY),
            (shaped((rows, heads * PAD, length), BF16), ANY),
            (shaped((tokens, width), BF16), ANY),
            (shaped((tokens, width), F32), ANY),
            (shaped((tokens, width), BF16), ANY),
            (shaped((width, 3 * width), BF16), ANY),
            (shaped((width, width), BF16), ANY),
        ],
        [SMEM, SMEM] + [VMEM] * 8 + [ANY] * n,
        [
            vm((width, 3 * width), BF16),
            vm((width, width), BF16),
            vm((tokens, width), BF16),
            vm((tokens, 3 * width), BF16),
            vm((rows * heads, length, length), BF16),
            vm((length, length), F32),
            vm((heads * PAD, length), F32),
            vm((rows, heads * PAD, length), BF16),
            vm((length, width), F32),
            vm((tokens, width), BF16),
            vm((tokens, width), F32),
            dma(len(triple_parts.parts) + len(output_parts.parts)),
            dma(8 + rows),
        ],
        8 * mm + 4 * rows * heads * length * length * HEAD,
        30 << 20,
    )(
        place,
        lengths,
        x,
        flat(gain_first),
        flat(shift_first),
        flat(output_bias),
        flat(gain_second),
        flat(shift_second),
        bdk,
        bdv,
        *first_arrays,
    )

    n = len(up_arrays)
    active, slope, up_full = call(
        partial(upward_body, up_parts, n),
        "upward",
        [
            (shaped((tokens, wide), BF16), ANY),
            (shaped((tokens, wide), BF16), ANY),
            (shaped((width, wide), BF16), ANY),
        ],
        [SMEM] + [VMEM] * 2 + [ANY] * n,
        [
            vm((width, wide), BF16),
            vm((tokens, wide), BF16),
            vm((tokens, wide), BF16),
            dma(len(up_parts.parts)),
            dma(3),
        ],
        8 * mm,
        25 << 20,
    )(place, norm_two, flat(upward_bias), *up_arrays)

    n = len(down_arrays)
    chunk_scratch = [
        vm((chunk, width), BF16),
        vm((width, chunk), BF16),
        vm((tokens, chunk), BF16),
        vm((tokens, chunk), BF16),
        vm((tokens, chunk), BF16),
        vm((tokens, width), F32),
        vm((tokens, width), F32),
    ]
    sums = [(shaped((tokens, width), F32), ANY)] * 2
    n_sems = len(down_parts.parts) + 4
    second, out = call(
        partial(chunk_body, (0,), True, down_parts, n),
        "chunk_own",
        sums,
        [SMEM, VMEM] + [ANY] * (3 + n),
        chunk_scratch + [dma(n_sems), dma(4)],
        6 * mm,
        12 << 20,
    )(place, g, active, slope, up_full, *down_arrays)
    second, out = call(
        partial(chunk_body, (1, 2), False, down_parts, n),
        "chunk_near",
        sums,
        [SMEM, VMEM] + [ANY] * (5 + n),
        chunk_scratch + [dma(n_sems), dma(4)],
        12 * mm,
        24 << 20,
    )(place, g, active, slope, up_full, *down_arrays, second, out)
    result, g_middle, g_mix, delta, d_pre, pairs = call(
        partial(middle_body, rows, (3,), down_parts, n),
        "middle",
        [
            (shaped((tokens, width), BF16), ANY),
            (shaped((tokens, width), F32), ANY),
            (shaped((tokens, width), BF16), ANY),
            (shaped((rows, heads * PAD, length), F32), VMEM),
            (shaped((rows, heads * PAD, length), BF16), VMEM),
            (shaped((2, PAD, width), F32), VMEM),
        ],
        [SMEM, VMEM]
        + [ANY] * (3 + n)
        + [ANY] * 3
        + [VMEM] * 2
        + [ANY]
        + [VMEM]
        + [ANY]
        + [VMEM] * 3,
        chunk_scratch
        + [
            vm((tokens, width), F32),
            vm((width, width), BF16),
            vm((tokens, width), BF16),
            vm((tokens, width), BF16),
            vm((tokens, width), BF16),
            vm((tokens, width), BF16),
            dma(n_sems),
            dma(8),
        ],
        9 * mm,
        24 << 20,
    )(
        place,
        g,
        active,
        slope,
        up_full,
        *down_arrays,
        second,
        out,
        middle,
        flat(gain_second),
        flat(downward_bias),
        output_full,
        mix,
        triple,
        pre,
        bdv,
        ones,
    )

    grads = []
    for row in range(rows):
        grads += call(
            partial(attend_back_body, row, length, heads),
            "attend_back_%d" % row,
            [(shaped((length, 3 * width), BF16), VMEM)],
            [ANY] * 3 + [VMEM] * 3,
            [
                vm((length, 3 * width), BF16),
                vm((length, width), BF16),
                vm((heads, length, length), BF16),
                dma(3),
            ],
            16 * heads * length * length * HEAD,
            8 << 20,
        )(triple, g_mix, prob, delta, d_pre, bdk)

    (input_grad,) = call(
        partial(input_body, rows),
        "input",
        [(shaped((tokens, width), BF16), VMEM)],
        [VMEM] * rows + [ANY] + [VMEM] * 2 + [ANY],
        [
            vm((width, 3 * width), BF16),
            vm((tokens, width), F32),
            vm((tokens, width), F32),
            dma(width // 256 + 1),
        ],
        6 * mm,
        13 << 20,
    )(*grads, triple_full, x, flat(gain_first), g_middle)

    pair_keys, pair_values = total_pairs(pairs, fsdp, dp)
    table_grad, inner_w_grad, inner_b_grad, outer_w_grad, outer_b_grad = call(
        partial(reparam_body, prefix),
        "reparam",
        [
            (shaped((PAD, width), F32), VMEM),
            (shaped((width, mid), F32), VMEM),
            (shaped((1, mid), F32), VMEM),
            (shaped((mid, 2 * width), F32), VMEM),
            (shaped((1, 2 * width), F32), VMEM),
        ],
        [VMEM] * 6,
        [],
        2 * PAD * mid * 6 * width,
        9 << 20,
    )(pair_keys, pair_values, hidden, table, inner_weight, outer_weight)
    return (
        result.reshape(rows, length, width),
        input_grad.reshape(rows, length, width),
        table_grad[:prefix],
        inner_w_grad,
        inner_b_grad.reshape(-1),
        outer_w_grad,
        outer_b_grad.reshape(-1),
    )


def solution(mesh):
    in_specs = (
        P(("dp", "fsdp"), None, None),
        P(("dp", "fsdp"), None),
        P(("dp", "fsdp"), None, None),
        P(),
        P(),
        P("fsdp", "dp"),
        P("fsdp", "dp"),
        P(),
        P(),
        P(),
        P("fsdp", "dp"),
        P(),
        P("fsdp", "dp"),
        P(),
        P(),
        P(),
        P(),
        P(),
        P(),
    )
    out_specs = (
        P(("dp", "fsdp"), None, None),
        P(("dp", "fsdp"), None, None),
        P(),
        P(),
        P(),
        P(),
        P(),
    )
    return jax.shard_map(
        partial(body, mesh.shape["fsdp"], mesh.shape["dp"]),
        mesh=mesh,
        in_specs=in_specs,
        out_specs=out_specs,
        check_vma=False,
    )
```

time: 835 us -> 314 us (0.38); the launches traced: 825 us -> 313 us
  waiting for transfers between devices: 570 us -> 113 us
  Pallas kernels: 0 us -> 130 us
  matrix products: 126 us -> 0 us
  blocking collectives: 52 us -> 0 us
  starting transfers between devices: 0.31 us -> 37.6 us
  local copies, waits for them, and re-layouts: 46.5 us -> 13.2 us
  other arithmetic: 14.4 us -> 5.85 us
    all_gather x7 -> x3, waiting for transfers between devices: 479 us -> 45.1 us  [foreign(): planes = lax.all_gather(value, 'dp', axis=0, tiled=False)]
    pallas_call x0 -> x10, Pallas kernels: none -> 130 us  [the longest x1 27.9 us: body(): call(partial(attend_body, rows, prefix, triple_parts, output_parts, n), '...]
    dot_general x32 -> x0, matrix products: 126 us -> none  [the longest x2 35.4 us: backward_row(): jnp.einsum('tf,df->td', upward_grad, upward_w, preferred_element_type=jnp...]
    psum x1 -> x0, waiting for transfers between devices: 89.3 us -> none  [body(): lax.psum((local_grads[0], local_grads[1], local_grads[2], local_grads[3],...]
    ppermute x0 -> x51, waiting for transfers between devices: none -> 66.2 us  [the longest x47 60.6 us: flip(): return lax.ppermute(value, 'fsdp', [(i, i ^ mask) for i in range(size)])]
    psum x1 -> x0, blocking collectives: 41.2 us -> none  [body(): lax.psum((local_grads[0], local_grads[1], local_grads[2], local_grads[3],...]
    ppermute x0 -> x51, starting transfers between devices: none -> 37.5 us  [the longest x47 31.8 us: flip(): return lax.ppermute(value, 'fsdp', [(i, i ^ mask) for i in range(size)])]
    slice x17 -> x10, local copies, waits for them, and re-layouts: 22.9 us -> 6.1 us  [the longest x5 3.05 us: spread(): diag_x = flip(along_y[:half], 2, size)]
  transfers between devices with their start and end apart: 8 -> 54, of which waited for: 8 -> 15; matrix products, arithmetic and copies ran while one was open for 10% -> 4% of each run, Pallas kernels for 0% -> 26%
where the time goes in v1:
time: 314 us; the launch traced here: 313 us
  Pallas kernels  130 us (41%)
  waiting for transfers between devices  113 us (36%)
  starting transfers between devices  37.6 us (12%)
  between operations  14.4 us (5%)
  local copies, waits for them, and re-layouts  13.2 us (4%)
  other arithmetic  5.85 us (2%)
    ppermute x47, waiting for transfers between devices, flip(): return lax.ppermute(value, 'fsdp', [(i, i ^ mask) for i in range(size)])  60.6 us
    all_gather x3, waiting for transfers between devices, foreign(): planes = lax.all_gather(value, 'dp', axis=0, tiled=False)  45.1 us
    ppermute x47, starting transfers between devices, flip(): return lax.ppermute(value, 'fsdp', [(i, i ^ mask) for i in range(size)])  31.8 us
    pallas_call x1, Pallas kernels, body(): call(partial(attend_body, rows, prefix, triple_parts, output_parts, n), '...  27.9 us
    pallas_call x2, Pallas kernels, body(): call(partial(attend_back_body, row, length, heads), 'attend_back_%d' % ro...  22.9 us
    pallas_call x1, Pallas kernels, body(): call(partial(upward_body, up_parts, n), 'upward', [(shaped((tokens, wide)...  18.1 us
    pallas_call x1, Pallas kernels, body(): call(partial(chunk_body, (1, 2), False, down_parts, n), 'chunk_near', sum...  16.6 us
    pallas_call x1, Pallas kernels, body(): call(partial(middle_body, rows, (3,), down_parts, n), 'middle', [(shaped(...  15.7 us
  transfers between devices with their start and end apart: 54, of which 15 were waited for; matrix products, arithmetic and copies ran while one was open for 4% of the time, Pallas kernels for 26%

profile of v1, /device:TPU:0, one launch (start us, length us, event | category | flops | bytes accessed | tf_op | source)
XLA Modules:
  0.0 313.5 jit_solution(8715344801386017580)
XLA Ops:
  7.2 1.7 pad_maximum_fusion.3
  11.5 3.0 collective-permute-start.1
  16.7 15.4 %collective-permute-done.28.refs_7_ = bf16[512,256]{1,0:T(8,128)(2,1)S(1)} collective-permute-done((bf16[512,256]{1,0:T(8,128)(2,1)S(1)}, bf16[512,256]{1,0:T(8,128)(2,1)S(1)}, u32[]{:S(2)}, u32[]{:S(2)}) %collective-permute-start.28) | collective-permute-done | bytes 262176 | tf_op jit(solution)/shard_map/ppermute | solution.py:120
  35.1 3.5 %collective-permute-done.29.refs_8_ = bf16[256,256]{1,0:T(8,128)(2,1)S(1)} collective-permute-done((bf16[256,256]{1,0:T(8,128)(2,1)S(1)}, bf16[256,256]{1,0:T(8,128)(2,1)S(1)}, u32[]{:S(2)}, u32[]{:S(2)}) %collective-permute-start.29) | collective-permute-done | bytes 131104 | tf_op jit(solution)/shard_map/ppermute | solution.py:120
  45.7 24.2 %all-gather.9.cloned.1.call-done = bf16[512,1024]{1,0:T(8,128)(2,1)} async-done(((bf16[128,1024]{1,0:T(8,128)(2,1)}), bf16[512,1024]{1,0:T(8,128)(2,1)}) %all-gather.9.cloned.1.call-update) | async-done | bytes 1048592 | tf_op jit(solution)/shard_map/all_gather | solution.py:146
  78.0 20.9 %all-gather.11.cloned.1.call-done = bf16[2048,256]{1,0:T(8,128)(2,1)} async-done(((bf16[512,256]{1,0:T(8,128)(2,1)}), bf16[2048,256]{1,0:T(8,128)(2,1)}) %all-gather.11.cloned.1.call-update) | async-done | bytes 1048592 | tf_op jit(solution)/shard_map/all_gather | solution.py:146
  102.2 8.4 %collective-permute-done.19.refs_15_ = bf16[384,1024]{1,0:T(8,128)(2,1)} collective-permute-done((bf16[384,1024]{1,0:T(8,128)(2,1)S(1)}, bf16[384,1024]{1,0:T(8,128)(2,1)}, u32[]{:S(2)}, u32[]{:S(2)}) %collective-permute-start.19) | collective-permute-done | bytes 786464 | tf_op jit(solution)/shard_map/ppermute | solution.py:120
  119.8 7.5 %collective-permute-done.37.refs_17_ = bf16[1536,256]{1,0:T(8,128)(2,1)S(1)} collective-permute-done((bf16[1536,256]{1,0:T(8,128)(2,1)S(1)}, bf16[1536,256]{1,0:T(8,128)(2,1)S(1)}, u32[]{:S(2)}, u32[]{:S(2)}) %collective-permute-start.37) | collective-permute-done | bytes 786464 | tf_op jit(solution)/shard_map/ppermute | solution.py:120
  128.8 2.2 collective-permute-done.36.refs_16_
  132.5 7.0 %collective-permute-done.11.refs_23_ = bf16[192,1024]{1,0:T(8,128)(2,1)S(1)} collective-permute-done((bf16[192,1024]{1,0:T(8,128)(2,1)S(1)}, bf16[192,1024]{1,0:T(8,128)(2,1)S(1)}, u32[]{:S(2)}, u32[]{:S(2)}) %collective-permute-start.11) | collective-permute-done | bytes 393248 | tf_op jit(solution)/shard_map/ppermute | solution.py:120
  140.1 7.9 %collective-permute-done.20.refs_16_ = bf16[192,1024]{1,0:T(8,128)(2,1)} collective-permute-done((bf16[192,1024]{1,0:T(8,128)(2,1)S(1)}, bf16[192,1024]{1,0:T(8,128)(2,1)}, u32[]{:S(2)}, u32[]{:S(2)}) %collective-permute-start.20) | collective-permute-done | bytes 393248 | tf_op jit(solution)/shard_map/ppermute | solution.py:120
  149.5 5.0 %collective-permute-done.38.refs_18_ = bf16[768,256]{1,0:T(8,128)(2,1)S(1)} collective-permute-done((bf16[768,256]{1,0:T(8,128)(2,1)S(1)}, bf16[768,256]{1,0:T(8,128)(2,1)S(1)}, u32[]{:S(2)}, u32[]{:S(2)}) %collective-permute-start.38) | collective-permute-done | bytes 393248 | tf_op jit(solution)/shard_map/ppermute | solution.py:120
  158.5 3.7 %prefix.1 = (f32[16,512]{1,0:T(8,128)}, bf16[256,1024]{1,0:T(8,128)(2,1)}, bf16[256,1024]{1,0:T(8,128)(2,1)}, bf16[256,1024]{1,0:T(8,128)(2,1)}) custom-call(bf16[16,1024]{1,0:T(8,128)(2,1)} %pad.4.table, bf16[1024,512]{1,0:T(8,128)(2,1)} %inner_w.3, f32[1,512]{1,0:T(1,128)} %bitcast.58, bf16[512,2048]{1,0:T(8,128)(2,1)} %outer_w.3, f32[1,2048]{1,0:T(1,128)} %bitcast.52), custom_call_target="tpu_custom_call" | custom-call | flops 50331648 | bytes 3145728 | tf_op jit(solution)/shard_map/prefix/pallas_call | solution.py:697
  163.3 27.9 %attend.1 = (bf16[512,3072]{1,0:T(8,128)(2,1)}, bf16[32,256,256]{2,1,0:T(8,128)(2,1)}, bf16[2,256,256]{2,1,0:T(8,128)(2,1)}, bf16[512,1024]{1,0:T(8,128)(2,1)}, ...) custom-call(s32[2]{0:T(128)} %pad_add_fusion.refs_0_, ...), custom_call_target="tpu_custom_call" | custom-call | flops 4831838208 | bytes 31457280 | tf_op jit(solution)/shard_map/attend/pallas_call | solution.py:708
  191.9 18.1 %upward.1 = (bf16[512,4096]{1,0:T(8,128)(2,1)}, bf16[512,4096]{1,0:T(8,128)(2,1)}, bf16[1024,4096]{1,0:T(8,128)(2,1)}) custom-call(s32[2]{0:T(128)} %pad_add_fusion.refs_0_, bf16[512,1024]{1,0:T(8,128)(2,1)} %get-tuple-element.39.refs_1_, f32[1,4096]{1,0:T(1,128)} %bitcast.61, bf16[128,2048]{1,0:T(8,128)(2,1)} %copy-done.23, ...), custom_call_target="tpu_custom_call" | custom-call | flops 4294967296 | bytes 26214400 | tf_op jit(solution)/shard_map/upward/pallas_call | solution.py:754
  211.6 9.2 %chunk_own.1 = (f32[512,1024]{1,0:T(8,128)}, f32[512,1024]{1,0:T(8,128)}) custom-call(s32[2]{0:T(128)} %pad_add_fusion.refs_0_, bf16[512,1024]{1,0:T(8,128)(2,1)} %bitcast.43, bf16[512,4096]{1,0:T(8,128)(2,1)} %get-tuple-element.40.refs_2_, bf16[512,4096]{1,0:T(8,128)(2,1)} %get-tuple-element.41.refs_3_, bf16[1024,4096]{1,0:T(8,128)(2,1)} %get-tuple-element.42.refs_4_, ...), custom_call_target="tpu_custom_call" | custom-call | flops 3221225472 | bytes 12582912 | tf_op jit(solution)/shard_map/chunk_own/pallas_call | solution.py:786
  220.8 16.6 %chunk_near.1 = (f32[512,1024]{1,0:T(8,128)}, f32[512,1024]{1,0:T(8,128)}) custom-call(s32[2]{0:T(128)} %pad_add_fusion.refs_0_, bf16[512,1024]{1,0:T(8,128)(2,1)} %bitcast.44, bf16[512,4096]{1,0:T(8,128)(2,1)} %get-tuple-element.40.refs_2_, bf16[512,4096]{1,0:T(8,128)(2,1)} %get-tuple-element.41.refs_3_, bf16[1024,4096]{1,0:T(8,128)(2,1)} %get-tuple-element.42.refs_4_, ...), custom_call_target="tpu_custom_call" | custom-call | flops 6442450944 | bytes 25165824 | tf_op jit(solution)/shard_map/chunk_near/pallas_call | solution.py:795
  237.5 15.7 %middle.1 = (bf16[512,1024]{1,0:T(8,128)(2,1)}, f32[512,1024]{1,0:T(8,128)}, bf16[512,1024]{1,0:T(8,128)(2,1)}, f32[2,256,256]{2,1,0:T(8,128)}, bf16[2,256,256]{2,1,0:T(8,128)(2,1)}, /*index=5*/f32[2,16,1024]{2,1,0:T(8,128)}) custom-call(s32[2]{0:T(128)} %pad_add_fusion.refs_0_, bf16[512,1024]{1,0:T(8,128)(2,1)} %bitcast.45, ...), custom_call_target="tpu_custom_call" | custom-call | flops 4831838208 | bytes 25165824 | tf_op jit(solution)/shard_map/middle/pallas_call | solution.py:804
  257.9 2.9 collective-permute-done.46
  262.4 2.8 collective-permute-done.47
  266.7 11.5 %attend_back_1.1.refs_1_ = bf16[256,3072]{1,0:T(8,128)(2,1)} custom-call(bf16[512,3072]{1,0:T(8,128)(2,1)} %get-tuple-element.50.refs_32_.triple, bf16[512,1024]{1,0:T(8,128)(2,1)} %get-tuple-element.54.gmix, bf16[32,256,256]{2,1,0:T(8,128)(2,1)} %get-tuple-element.55.prob, f32[2,256,256]{2,1,0:T(8,128)} %get-tuple-element.56.delta, ...), custom_call_target="tpu_custom_call" | custom-call | flops 1073741824 | bytes 8388608 | tf_op jit(solution)/shard_map/attend_back_1/pallas_call | solution.py:858
  279.3 11.4 %attend_back_0.1.refs_0_ = bf16[256,3072]{1,0:T(8,128)(2,1)} custom-call(bf16[512,3072]{1,0:T(8,128)(2,1)} %get-tuple-element.50.refs_32_.triple, bf16[512,1024]{1,0:T(8,128)(2,1)} %get-tuple-element.54.gmix, bf16[32,256,256]{2,1,0:T(8,128)(2,1)} %get-tuple-element.55.prob, f32[2,256,256]{2,1,0:T(8,128)} %get-tuple-element.56.delta, ...), custom_call_target="tpu_custom_call" | custom-call | flops 1073741824 | bytes 8388608 | tf_op jit(solution)/shard_map/attend_back_0/pallas_call | solution.py:858
  290.8 10.0 %input.1 = bf16[512,1024]{1,0:T(8,128)(2,1)} custom-call(bf16[256,3072]{1,0:T(8,128)(2,1)} %attend_back_0.1.refs_0_, bf16[256,3072]{1,0:T(8,128)(2,1)} %attend_back_1.1.refs_1_, bf16[1024,3072]{1,0:T(8,128)(2,1)} %get-tuple-element.58.refs_2_, bf16[512,1024]{1,0:T(8,128)(2,1)} %bitcast.47, f32[1,1024]{1,0:T(1,128)} %bitcast.54, ...), custom_call_target="tpu_custom_call" | custom-call | flops 3221225472 | bytes 13631488 | tf_op jit(solution)/shard_map/input/pallas_call | solution.py:873
  301.5 5.5 %reparam.1 = (f32[16,1024]{1,0:T(8,128)}, f32[1024,512]{1,0:T(8,128)}, f32[1,512]{1,0:T(1,128)}, f32[512,2048]{1,0:T(8,128)}, f32[1,2048]{1,0:T(1,128)}) custom-call(f32[16,1024]{1,0:T(8,128)} %get-tuple-element.77.keys, f32[16,1024]{1,0:T(8,128)} %get-tuple-element.76.values, f32[16,512]{1,0:T(8,128)} %get-tuple-element.61.hidden_r, ...), custom_call_target="tpu_custom_call" | custom-call | flops 100663296 | bytes 9437184 | tf_op jit(solution)/shard_map/reparam/pallas_call | solution.py:889
  (195 shorter events, 57.1 us)
Async XLA Ops:
  7.2 38.5 %all-gather.7.cloned.1.call-start = ((), (), s32[]{:S(2)}) async-start(), calls=%async_computation | async-start | bytes 1310720 | tf_op jit(solution)/shard_map/all_gather | solution.py:146
  9.0 60.9 %all-gather.9.cloned.1.call-start = ((), (), s32[]{:S(2)}) async-start(), calls=%async_computation.1 | async-start | bytes 1310720 | tf_op jit(solution)/shard_map/all_gather | solution.py:146
  9.8 89.1 %all-gather.11.cloned.1.call-start = ((), (), s32[]{:S(2)}) async-start(), calls=%async_computation.2 | async-start | bytes 1310720 | tf_op jit(solution)/shard_map/all_gather | solution.py:146
  11.5 28.3 %collective-permute-start.1 = (bf16[128,2048]{1,0:T(8,128)(2,1)S(1)}, bf16[128,2048]{1,0:T(8,128)(2,1)}, u32[]{:S(2)}, u32[]{:S(2)}) collective-permute-start(bf16[128,2048]{1,0:T(8,128)(2,1)S(1)} %constant_dynamic-update-slice_fusion.refs_10_.refs_3_), channel_id=1, source_target_pairs={{0,4},{1,5},{2,6},{3,7},{4,0},{5,1},{6,2},{7,3},{8,12},{9,13},{10,... | collective-permute-start | bytes 1572872 | tf_op jit(solution)/shard_map/ppermute | solution.py:120
  14.6 26.3 %collective-permute-start = (bf16[128,2048]{1,0:T(8,128)(2,1)S(1)}, bf16[128,2048]{1,0:T(8,128)(2,1)}, u32[]{:S(2)}, u32[]{:S(2)}) collective-permute-start(bf16[128,2048]{1,0:T(8,128)(2,1)S(1)} %constant_dynamic-update-slice_fusion.refs_10_.refs_3_), channel_id=1, source_target_pairs={{0,2},{1,3},{2,0},{3,1},{4,6},{5,7},{6,4},{7,5},{8,10},{9,11},{10,... | collective-permute-start | bytes 1572872 | tf_op jit(solution)/shard_map/ppermute | solution.py:120
  16.7 27.3 %collective-permute-start.4 = (bf16[128,2048]{1,0:T(8,128)(2,1)S(1)}, bf16[128,2048]{1,0:T(8,128)(2,1)S(1)}, u32[]{:S(2)}, u32[]{:S(2)}) collective-permute-start(bf16[128,2048]{1,0:T(8,128)(2,1)S(1)} %constant_dynamic-update-slice_fusion.refs_10_.refs_3_), channel_id=1, source_target_pairs={{0,1},{1,0},{2,3},{3,2},{4,5},{5,4},{6,7},{7,6},{8,9},{9,8},{10,11... | collective-permute-start | bytes 1572872 | tf_op jit(solution)/shard_map/ppermute | solution.py:120
  40.8 30.7 %collective-permute-start.2 = (bf16[64,2048]{1,0:T(8,128)(2,1)S(1)}, bf16[64,2048]{1,0:T(8,128)(2,1)}, u32[]{:S(2)}, u32[]{:S(2)}) collective-permute-start(bf16[64,2048]{1,0:T(8,128)(2,1)S(1)} %slice.54), channel_id=1, source_target_pairs={{0,2},{1,3},{2,0},{3,1},{4,6},{5,7},{6,4},{7,5},{8,10},{9,11},{10,... | collective-permute-start | bytes 786440 | tf_op jit(solution)/shard_map/ppermute | solution.py:120
  43.4 29.7 %collective-permute-start.32 = (bf16[512,256]{1,0:T(8,128)(2,1)S(1)}, bf16[512,256]{1,0:T(8,128)(2,1)S(1)}, u32[]{:S(2)}, u32[]{:S(2)}) collective-permute-start(bf16[512,256]{1,0:T(8,128)(2,1)S(1)} %collective-permute-done.27.refs_6_), channel_id=1, source_target_pairs={{0,1},{1,0},{2,3},{3,2},{4,5},{5,4},{6,7},{7,6},{8,9},{9,8},{10,11... | collective-permute-start | bytes 786440 | tf_op jit(solution)/shard_map/ppermute | solution.py:120
  43.7 30.9 %collective-permute-start.33 = (bf16[512,256]{1,0:T(8,128)(2,1)S(1)}, bf16[512,256]{1,0:T(8,128)(2,1)S(1)}, u32[]{:S(2)}, u32[]{:S(2)}) collective-permute-start(bf16[512,256]{1,0:T(8,128)(2,1)S(1)} %collective-permute-done.28.refs_7_), channel_id=1, source_target_pairs={{0,1},{1,0},{2,3},{3,2},{4,5},{5,4},{6,7},{7,6},{8,9},{9,8},{10,11... | collective-permute-start | bytes 786440 | tf_op jit(solution)/shard_map/ppermute | solution.py:120
  44.0 27.5 %collective-permute-start.35 = (bf16[256,256]{1,0:T(8,128)(2,1)S(1)}, bf16[256,256]{1,0:T(8,128)(2,1)S(1)}, u32[]{:S(2)}, u32[]{:S(2)}) collective-permute-start(bf16[256,256]{1,0:T(8,128)(2,1)S(1)} %collective-permute-done.30.refs_9_), channel_id=1, source_target_pairs={{0,1},{1,0},{2,3},{3,2},{4,5},{5,4},{6,7},{7,6},{8,9},{9,8},{10,11... | collective-permute-start | bytes 393224 | tf_op jit(solution)/shard_map/ppermute | solution.py:120
  44.3 28.7 %collective-permute-start.3 = (bf16[64,2048]{1,0:T(8,128)(2,1)S(1)}, bf16[64,2048]{1,0:T(8,128)(2,1)}, u32[]{:S(2)}, u32[]{:S(2)}) collective-permute-start(bf16[64,2048]{1,0:T(8,128)(2,1)S(1)} %slice.55), channel_id=1, source_target_pairs={{0,4},{1,5},{2,6},{3,7},{4,0},{5,1},{6,2},{7,3},{8,12},{9,13},{10,... | collective-permute-start | bytes 786440 | tf_op jit(solution)/shard_map/ppermute | solution.py:120
  73.1 27.2 %collective-permute-start.10 = (bf16[384,1024]{1,0:T(8,128)(2,1)}, bf16[384,1024]{1,0:T(8,128)(2,1)}, u32[]{:S(2)}, u32[]{:S(2)}) collective-permute-start(bf16[384,1024]{1,0:T(8,128)(2,1)} %pad_maximum_fusion.refs_20_), channel_id=1, source_target_pairs={{0,4},{1,5},{2,6},{3,7},{4,0},{5,1},{6,2},{7,3},{8,12},{9,13},{10,... | collective-permute-start | bytes 2359304 | tf_op jit(solution)/shard_map/ppermute | solution.py:120
  74.6 26.2 %collective-permute-start.9 = (bf16[384,1024]{1,0:T(8,128)(2,1)}, bf16[384,1024]{1,0:T(8,128)(2,1)}, u32[]{:S(2)}, u32[]{:S(2)}) collective-permute-start(bf16[384,1024]{1,0:T(8,128)(2,1)} %pad_maximum_fusion.refs_20_), channel_id=1, source_target_pairs={{0,2},{1,3},{2,0},{3,1},{4,6},{5,7},{6,4},{7,5},{8,10},{9,11},{10,... | collective-permute-start | bytes 2359304 | tf_op jit(solution)/shard_map/ppermute | solution.py:120
  76.1 34.5 %collective-permute-start.19 = (bf16[384,1024]{1,0:T(8,128)(2,1)S(1)}, bf16[384,1024]{1,0:T(8,128)(2,1)}, u32[]{:S(2)}, u32[]{:S(2)}) collective-permute-start(bf16[384,1024]{1,0:T(8,128)(2,1)S(1)} %pad_maximum_fusion.1.refs_13_), channel_id=1, source_target_pairs={{0,4},{1,5},{2,6},{3,7},{4,0},{5,1},{6,2},{7,3},{8,12},{9,13},{10,... | collective-permute-start | bytes 2359304 | tf_op jit(solution)/shard_map/ppermute | solution.py:120
  77.5 35.6 %collective-permute-start.18 = (bf16[384,1024]{1,0:T(8,128)(2,1)S(1)}, bf16[384,1024]{1,0:T(8,128)(2,1)}, u32[]{:S(2)}, u32[]{:S(2)}) collective-permute-start(bf16[384,1024]{1,0:T(8,128)(2,1)S(1)} %pad_maximum_fusion.1.refs_13_), channel_id=1, source_target_pairs={{0,2},{1,3},{2,0},{3,1},{4,6},{5,7},{6,4},{7,5},{8,10},{9,11},{10,... | collective-permute-start | bytes 2359304 | tf_op jit(solution)/shard_map/ppermute | solution.py:120
  100.8 26.6 %collective-permute-start.37 = (bf16[1536,256]{1,0:T(8,128)(2,1)S(1)}, bf16[1536,256]{1,0:T(8,128)(2,1)S(1)}, u32[]{:S(2)}, u32[]{:S(2)}) collective-permute-start(bf16[1536,256]{1,0:T(8,128)(2,1)S(1)} %pad_maximum_fusion.2.refs_15_), channel_id=1, source_target_pairs={{0,4},{1,5},{2,6},{3,7},{4,0},{5,1},{6,2},{7,3},{8,12},{9,13},{10,... | collective-permute-start | bytes 2359304 | tf_op jit(solution)/shard_map/ppermute | solution.py:120
  113.1 26.4 %collective-permute-start.11 = (bf16[192,1024]{1,0:T(8,128)(2,1)S(1)}, bf16[192,1024]{1,0:T(8,128)(2,1)S(1)}, u32[]{:S(2)}, u32[]{:S(2)}) collective-permute-start(bf16[192,1024]{1,0:T(8,128)(2,1)S(1)} %slice.56), channel_id=1, source_target_pairs={{0,2},{1,3},{2,0},{3,1},{4,6},{5,7},{6,4},{7,5},{8,10},{9,11},{10,... | collective-permute-start | bytes 1179656 | tf_op jit(solution)/shard_map/ppermute | solution.py:120
  118.4 29.6 %collective-permute-start.20 = (bf16[192,1024]{1,0:T(8,128)(2,1)S(1)}, bf16[192,1024]{1,0:T(8,128)(2,1)}, u32[]{:S(2)}, u32[]{:S(2)}) collective-permute-start(bf16[192,1024]{1,0:T(8,128)(2,1)S(1)} %slice.58), channel_id=1, source_target_pairs={{0,2},{1,3},{2,0},{3,1},{4,6},{5,7},{6,4},{7,5},{8,10},{9,11},{10,... | collective-permute-start | bytes 1179656 | tf_op jit(solution)/shard_map/ppermute | solution.py:120
  131.1 23.4 %collective-permute-start.38 = (bf16[768,256]{1,0:T(8,128)(2,1)S(1)}, bf16[768,256]{1,0:T(8,128)(2,1)S(1)}, u32[]{:S(2)}, u32[]{:S(2)}) collective-permute-start(bf16[768,256]{1,0:T(8,128)(2,1)S(1)} %slice.62), channel_id=1, source_target_pairs={{0,2},{1,3},{2,0},{3,1},{4,6},{5,7},{6,4},{7,5},{8,10},{9,11},{10,... | collective-permute-start | bytes 1179656 | tf_op jit(solution)/shard_map/ppermute | solution.py:120
  156.6 34.6 %collective-permute-start.23 = (bf16[384,1024]{1,0:T(8,128)(2,1)}, bf16[384,1024]{1,0:T(8,128)(2,1)}, u32[]{:S(2)}, u32[]{:S(2)}) collective-permute-start(bf16[384,1024]{1,0:T(8,128)(2,1)} %collective-permute-done.18.refs_14_), channel_id=1, source_target_pairs={{0,1},{1,0},{2,3},{3,2},{4,5},{5,4},{6,7},{7,6},{8,9},{9,8},{10,11... | collective-permute-start | bytes 2359304 | tf_op jit(solution)/shard_map/ppermute | solution.py:120
  157.4 34.4 %collective-permute-start.24 = (bf16[384,1024]{1,0:T(8,128)(2,1)}, bf16[384,1024]{1,0:T(8,128)(2,1)}, u32[]{:S(2)}, u32[]{:S(2)}) collective-permute-start(bf16[384,1024]{1,0:T(8,128)(2,1)} %collective-permute-done.19.refs_15_), channel_id=1, source_target_pairs={{0,1},{1,0},{2,3},{3,2},{4,5},{5,4},{6,7},{7,6},{8,9},{9,8},{10,11... | collective-permute-start | bytes 2359304 | tf_op jit(solution)/shard_map/ppermute | solution.py:120
  162.7 47.2 %collective-permute-start.40 = (bf16[1536,256]{1,0:T(8,128)(2,1)S(1)}, bf16[1536,256]{1,0:T(8,128)(2,1)S(1)}, u32[]{:S(2)}, u32[]{:S(2)}) collective-permute-start(bf16[1536,256]{1,0:T(8,128)(2,1)S(1)} %pad_maximum_fusion.2.refs_15_), channel_id=1, source_target_pairs={{0,1},{1,0},{2,3},{3,2},{4,5},{5,4},{6,7},{7,6},{8,9},{9,8},{10,11... | collective-permute-start | bytes 2359304 | tf_op jit(solution)/shard_map/ppermute | solution.py:120
  162.8 47.2 %collective-permute-start.41 = (bf16[1536,256]{1,0:T(8,128)(2,1)S(1)}, bf16[1536,256]{1,0:T(8,128)(2,1)S(1)}, u32[]{:S(2)}, u32[]{:S(2)}) collective-permute-start(bf16[1536,256]{1,0:T(8,128)(2,1)S(1)} %collective-permute-done.36.refs_16_), channel_id=1, source_target_pairs={{0,1},{1,0},{2,3},{3,2},{4,5},{5,4},{6,7},{7,6},{8,9},{9,8},{10,11... | collective-permute-start | bytes 2359304 | tf_op jit(solution)/shard_map/ppermute | solution.py:120
  163.3 46.8 %collective-permute-start.42 = (bf16[1536,256]{1,0:T(8,128)(2,1)S(1)}, bf16[1536,256]{1,0:T(8,128)(2,1)S(1)}, u32[]{:S(2)}, u32[]{:S(2)}) collective-permute-start(bf16[1536,256]{1,0:T(8,128)(2,1)S(1)} %collective-permute-done.37.refs_17_), channel_id=1, source_target_pairs={{0,1},{1,0},{2,3},{3,2},{4,5},{5,4},{6,7},{7,6},{8,9},{9,8},{10,11... | collective-permute-start | bytes 2359304 | tf_op jit(solution)/shard_map/ppermute | solution.py:120
  (65 other events, 1173.2 us)
Sparse Core Ops, SparseCore 0:
  10.2 30.6 all-gather.6
  42.4 27.4 all-gather.8
  71.4 27.4 all-gather.10
